TPU v7x, 32 devices: a whole 2x2x4 slice. The times are simulated.
32 devices in a mesh: row: 8 (over z, x), col: 4 (over y, core).
Axes of the slice: x: 2, y: 2, z: 4, core: 2. Of those that a mesh axis runs over, the one named last changes fastest.
Arguments:
- queries: bfloat16 [64, 64, 768], P('row', 'col'), may hold values from -6 to 6
- keys: bfloat16 [64, 64, 768], P('row', 'col'), may hold values from -6 to 6
- values: bfloat16 [64, 64, 768], P('row', 'col'), may hold values from -6 to 6
- d_out: bfloat16 [64, 64, 768], P('row', 'col'), may hold values from -6 to 6
- extents: int32 [2, 4, 4], replicated, may hold values from 4 to 16, as said below
- rel_bias: float32 [12, 13, 13], replicated, may hold values from -4 to 4
Outputs:
- attended: bfloat16 [64, 64, 768], P('row', 'col')
- d_queries: bfloat16 [64, 64, 768], P('row', 'col')
- d_keys: bfloat16 [64, 64, 768], P('row', 'col')
- d_values: bfloat16 [64, 64, 768], P('row', 'col')
- d_rel_bias: float32 [12, 13, 13], replicated
Inputs may be any that keep to these rules, and one draw needn't show every extreme that they name: `extents`: every slot holds one image at its top-left corner.
All inputs are finite; a program needn't handle non-finite values.
Results may differ from a plain program's by a relative error of at most 0.011.
Values may be sent and summed in bfloat16 or wider, within the bound.
A program may use at most 64 MiB of HBM per device.

v0:
```python
import functools

import jax
import jax.numpy as jnp
from jax import lax
from jax.experimental import pallas as pl
from jax.experimental.pallas import tpu as pltpu
from jax.sharding import PartitionSpec as P

MESH = pl.DeviceIdType.MESH
F32 = jnp.float32
BF16 = jnp.bfloat16
CHUNKS = 3
NEG = -1e30


def nt(a, b):
    return lax.dot_general(a, b, (((1,), (1,)), ((), ())), preferred_element_type=F32)


def nn(a, b):
    return lax.dot_general(a, b, (((1,), (0,)), ((), ())), preferred_element_type=F32)


def halves(x):
    high = x.astype(BF16)
    low = (x - high.astype(F32)).astype(BF16)
    return jnp.concatenate([high, low], axis=0)


def kernel(
    n_row, n_col, tr, tc, rad,
    q_ref, k_ref, v_ref, g_ref, ext_ref, rel_ref,
    o_ref, dq_ref, dk_ref, dv_ref, rb_ref,
    kv, pack, bias, mask, table, dtable, centre, strip_out, strip_in, rows_out, rows_in,
    part, slots_r, slots_c,
    kr_s, kr_r, kc_s, kc_r, gc_s, gc_r, gr_s, gr_r, br_s, br_r, bc_s, bc_r,
):
    row, col = lax.axis_index("row"), lax.axis_index("col")
    nk = tr + 2 * rad
    nq = tr * tc
    half = tc // 2
    mid, side = nk * tc, nk * half
    halo = rad * tc
    chunks, _, keys, wide = kv.shape
    per = wide // 128
    pairs = chunks * per
    panels_r, panels_c = ext_ref.shape[1], ext_ref.shape[2]
    panel = 2 * tr

    up, down = row > 0, row < n_row - 1
    left, right = col > 0, col < n_col - 1
    row_down, row_up = lax.rem(row + 1, n_row), lax.rem(row + n_row - 1, n_row)
    col_right, col_left = lax.rem(col + 1, n_col), lax.rem(col + n_col - 1, n_col)

    barrier = pltpu.get_barrier_semaphore()
    for step in range(1, n_row):
        pl.semaphore_signal(
            barrier, inc=1, device_id=(lax.rem(row + step, n_row), col), device_id_type=MESH
        )
    for step in range(1, n_col):
        pl.semaphore_signal(
            barrier, inc=1, device_id=(row, lax.rem(col + step, n_col)), device_id_type=MESH
        )

    for c in range(chunks):
        kv[c, 0, halo : halo + nq, :] = k_ref[:, c * wide : (c + 1) * wide]
        kv[c, 1, halo : halo + nq, :] = v_ref[:, c * wide : (c + 1) * wide]
    pl.semaphore_wait(barrier, n_row - 1 + n_col - 1)

    def remote(src, dst, send, recv, to):
        return pltpu.make_async_remote_copy(
            src_ref=src, dst_ref=dst, send_sem=send, recv_sem=recv, device_id=to, device_id_type=MESH
        )

    def key_rows(c):
        return (
            remote(kv.at[c, :, nq + halo - halo : nq + halo], kv.at[c, :, 0:halo],
                   kr_s.at[c, 0], kr_r.at[c, 0], (row_down, col)),
            remote(kv.at[c, :, halo : 2 * halo], kv.at[c, :, halo + nq : mid],
                   kr_s.at[c, 1], kr_r.at[c, 1], (row_up, col)),
        )

    def key_cols(c):
        return (
            remote(pack.at[c, :, 0:side], kv.at[c, :, mid : mid + side],
                   kc_s.at[c, 0], kc_r.at[c, 0], (row, col_right)),
            remote(pack.at[c, :, side : 2 * side], kv.at[c, :, mid + side : mid + 2 * side],
                   kc_s.at[c, 1], kc_r.at[c, 1], (row, col_left)),
        )

    def grad_cols(c):
        return (
            remote(strip_out.at[c, :, side : 2 * side], strip_in.at[c, :, side : 2 * side],
                   gc_s.at[c, 0], gc_r.at[c, 0], (row, col_right)),
            remote(strip_out.at[c, :, 0:side], strip_in.at[c, :, 0:side],
                   gc_s.at[c, 1], gc_r.at[c, 1], (row, col_left)),
        )

    def grad_rows(c):
        return (
            remote(rows_out.at[c, :, halo : 2 * halo], rows_in.at[c, :, halo : 2 * halo],
                   gr_s.at[c, 0], gr_r.at[c, 0], (row_down, col)),
            remote(rows_out.at[c, :, 0:halo], rows_in.at[c, :, 0:halo],
                   gr_s.at[c, 1], gr_r.at[c, 1], (row_up, col)),
        )

    def start(copies, after, before):
        pl.when(after)(lambda: copies[0].start())
        pl.when(before)(lambda: copies[1].start())

    def arrive(copies, after, before):
        pl.when(before)(lambda: copies[0].wait_recv())
        pl.when(after)(lambda: copies[1].wait_recv())

    def sent(copies, after, before):
        pl.when(after)(lambda: copies[0].wait_send())
        pl.when(before)(lambda: copies[1].wait_send())

    for c in range(chunks):
        start(key_rows(c), down, up)

    @pl.when(jnp.logical_not(up))
    def _():
        kv[:, :, 0:halo, :] = jnp.zeros((chunks, 2, halo, wide), BF16)
        rows_in[:, :, halo : 2 * halo, :] = jnp.zeros((chunks, 2, halo, wide), BF16)

    @pl.when(jnp.logical_not(down))
    def _():
        kv[:, :, halo + nq : mid, :] = jnp.zeros((chunks, 2, halo, wide), BF16)
        rows_in[:, :, 0:halo, :] = jnp.zeros((chunks, 2, halo, wide), BF16)

    @pl.when(jnp.logical_not(left))
    def _():
        kv[:, :, mid : mid + side, :] = jnp.zeros((chunks, 2, side, wide), BF16)
        strip_in[:, :, side : 2 * side, :] = jnp.zeros((chunks, 2, side, wide), BF16)

    @pl.when(jnp.logical_not(right))
    def _():
        kv[:, :, mid + side : mid + 2 * side, :] = jnp.zeros((chunks, 2, side, wide), BF16)
        strip_in[:, :, 0:side, :] = jnp.zeros((chunks, 2, side, wide), BF16)

    tiles_n = table.shape[0]
    span_lanes = tiles_n * 128
    heads_pad = rel_ref.shape[0]
    cols2 = 2 * tc

    def one_hot(kc):
        lane = lax.broadcasted_iota(jnp.int32, (1, span_lanes), 1)
        a = nk - 1 - lane // tc
        b = kc - (half - rad) - lane % tc
        target = jnp.where((a >= 0) & (a < 16) & (b >= 0) & (b < 16), a * 16 + b, -1)
        place = lax.broadcasted_iota(jnp.int32, (256, span_lanes), 0)
        return jnp.where(place == target, 1.0, 0.0).astype(BF16)

    rel2 = halves(rel_ref[...])

    def fill_table(kc, carry):
        both = nn(rel2, one_hot(kc))
        both = both[:heads_pad] + both[heads_pad:]
        for t in range(tiles_n):
            table[t, pl.ds(kc, heads_pad, stride=cols2), :] = both[:, t * 128 : (t + 1) * 128]
        return carry

    lax.fori_loop(0, cols2, fill_table, 0)

    sub = lax.broadcasted_iota(jnp.int32, (cols2, nq), 0)
    lane = lax.broadcasted_iota(jnp.int32, (cols2, nq), 1)
    q_row, q_col = lane // tc, lane % tc
    q_high = ext_ref[0, (row * tr) // panel, col]
    q_wide = ext_ref[1, (row * tr) // panel, col]
    q_first = lax.rem(row * tr, panel)
    col_diff = sub - (half - rad) - q_col
    fits = (
        (q_row + q_first < q_high) & (q_col < q_wide) & (col_diff >= 0) & (col_diff <= 2 * rad)
    )
    col_mod = lax.rem(sub + half, tc)
    for kr in range(nk):
        r = row * tr - rad + kr
        inside = (r >= 0) & (r < n_row * tr)
        pr = jnp.clip(r, 0, n_row * tr - 1) // panel
        widths = []
        for shift in (-1, 0, 1):
            pc = jnp.clip(col + shift, 0, panels_c - 1)
            there = inside & (col + shift >= 0) & (col + shift < n_col)
            there = there & (r - pr * panel < ext_ref[0, pr, pc])
            widths.append(jnp.where(there, ext_ref[1, pr, pc], 0))
        width = jnp.where(
            sub < half, widths[0], jnp.where(sub < half + tc, widths[1], widths[2])
        )
        row_diff = kr - q_row
        allowed = fits & (row_diff >= 0) & (row_diff <= 2 * rad) & (col_mod < width)
        mask[kr] = jnp.where(allowed, 0.0, NEG)

    def fill_bias(p, carry):
        for hh in range(2):
            base = pl.multiple_of((p * 2 + hh) * cols2, cols2)
            tiles = [table[t, pl.ds(base, cols2), :] for t in range(tiles_n)]
            lo = hh * 128
            for kr in range(nk):
                off = (nk - 1 - kr) * tc
                t, s = off // 128, off % 128
                x = tiles[t]
                if s:
                    x = pltpu.roll(jnp.where(lane >= s, x, tiles[t + 1]), 128 - s, 1)
                x = x + mask[kr]
                bias[p, mid + kr * half : mid + (kr + 1) * half, lo : lo + 128] = x[:half]
                bias[p, kr * tc : (kr + 1) * tc, lo : lo + 128] = x[half : half + tc]
                at = mid + side + kr * half
                bias[p, at : at + half, lo : lo + 128] = x[half + tc :]
        return carry

    lax.fori_loop(0, pairs, fill_bias, 0)

    q_sub = lax.broadcasted_iota(jnp.int32, (nq, 128), 0)
    ch = lax.broadcasted_iota(jnp.int32, (nq, 128), 1)
    q_valid = (q_sub // tc + q_first < q_high) & (q_sub % tc < q_wide)

    def send_cols(c):
        arrive(key_rows(c), down, up)
        for i in range(2):
            x = kv[c, i, 0:mid, :].astype(F32).reshape(nk, tc, wide)
            pack[c, i, 0:side, :] = x[:, half:].reshape(side, wide).astype(BF16)
            pack[c, i, side : 2 * side, :] = x[:, :half].reshape(side, wide).astype(BF16)
        start(key_cols(c), right, left)

    def block(x):
        zero = jnp.zeros_like(x)
        return jnp.concatenate(
            [jnp.where(ch < 64, x, zero), jnp.where(ch < 64, zero, x)], axis=0
        ).astype(BF16)

    def compute(c, pp):
        p = c * per + pp
        at = pl.multiple_of(pp * 128, 128)
        full = pl.multiple_of(p * 128, 128)
        k2 = kv[c, 0, :, pl.ds(at, 128)]
        v2 = kv[c, 1, :, pl.ds(at, 128)]
        qb = block(q_ref[:, pl.ds(full, 128)].astype(F32) * 0.125)
        gb = block(jnp.where(q_valid, g_ref[:, pl.ds(full, 128)].astype(F32), 0.0))
        score = nt(k2, qb) + bias[p]
        weights = jnp.exp(score - jnp.max(score, axis=0, keepdims=True))
        prob = weights * (1.0 / jnp.sum(weights, axis=0, keepdims=True))
        prob_b = prob.astype(BF16)
        dprob = nt(v2, gb)
        delta = jnp.sum(prob_b.astype(F32) * dprob, axis=0, keepdims=True)
        ds = prob * (dprob - delta)
        ds_b = ds.astype(BF16)

        def back(x, scores):
            both = nn(x.T, scores)
            return jnp.concatenate([both[:64, :128], both[64:, 128:]], axis=0).T

        o_ref[:, pl.ds(full, 128)] = jnp.where(q_valid, back(v2, prob_b), 0.0).astype(BF16)
        dq_ref[:, pl.ds(full, 128)] = (back(k2, ds_b) * 0.125).astype(BF16)
        for i, grad in enumerate((nn(ds_b, qb), nn(prob_b, gb))):
            centre[c, i, :, pl.ds(at, 128)] = grad[:mid]
            strip_out[c, i, :, pl.ds(at, 128)] = grad[mid:].astype(BF16)
        for hh in range(2):
            d = ds[:, hh * 128 : (hh + 1) * 128]
            sums = [jnp.zeros((cols2, nq), F32) for _ in range(tiles_n)]
            for kr in range(nk):
                off = (nk - 1 - kr) * tc
                t, s = off // 128, off % 128
                at2 = mid + kr * half
                x = jnp.concatenate(
                    [d[at2 : at2 + half], d[kr * tc : (kr + 1) * tc],
                     d[side + at2 : side + at2 + half]], axis=0,
                )
                if s:
                    x = pltpu.roll(x, s, 1)
                    sums[t] = sums[t] + jnp.where(lane >= s, x, 0.0)
                    sums[t + 1] = sums[t + 1] + jnp.where(lane >= s, 0.0, x)
                else:
                    sums[t] = sums[t] + x
            base = pl.multiple_of((p * 2 + hh) * cols2, cols2)
            for t, total in enumerate(sums):
                dtable[t, pl.ds(base, cols2), :] = total

    def send_rows(c):
        arrive(grad_cols(c), right, left)
        for i in range(2):
            x = centre[c, i].reshape(nk, tc, wide)
            y = jnp.concatenate(
                [strip_in[c, i, side : 2 * side, :].astype(F32).reshape(nk, half, wide),
                 strip_in[c, i, 0:side, :].astype(F32).reshape(nk, half, wide)], axis=1,
            )
            total = (x + y).reshape(mid, wide)
            rows_out[c, i, 0:halo, :] = total[:halo].astype(BF16)
            rows_out[c, i, halo : 2 * halo, :] = total[halo + nq :].astype(BF16)
            centre[c, i, halo : halo + nq, :] = total[halo : halo + nq]
        start(grad_rows(c), down, up)

    send_cols(0)
    for c in range(chunks):
        if c + 1 < chunks:
            send_cols(c + 1)
        arrive(key_cols(c), right, left)

        def one(pp, carry, c=c):
            compute(c, pp)
            return carry

        lax.fori_loop(0, per, one, 0)
        start(grad_cols(c), right, left)
        if c:
            send_rows(c - 1)
    unused = heads_pad - pairs * 2
    dtable[:, pairs * 2 * cols2 :, :] = jnp.zeros((tiles_n, unused * cols2, 128), F32)

    def gather_bias(kc, total):
        x = jnp.concatenate(
            [dtable[t, pl.ds(kc, heads_pad, stride=cols2), :] for t in range(tiles_n)], axis=1
        )
        both = nt(halves(x), one_hot(kc))
        return total + both[:heads_pad] + both[heads_pad:]

    part[...] = lax.fori_loop(0, cols2, gather_bias, jnp.zeros((heads_pad, 256), F32))

    def spread(slots, me, count, send, recv, to):
        copies = [
            remote(part, slots.at[me], send.at[k], recv.at[k], to(lax.rem(me + k, count)))
            for k in range(1, count)
        ]
        return copies

    over_rows = spread(slots_r, row, n_row, br_s, br_r, lambda r: (r, col))
    for copy in over_rows:
        copy.start()
    slots_r[row] = part[...]
    send_rows(chunks - 1)
    for copy in over_rows:
        copy.wait()
    total = slots_r[0]
    for k in range(1, n_row):
        total = total + slots_r[k]
    part[...] = total
    over_cols = spread(slots_c, col, n_col, bc_s, bc_r, lambda k: (row, k))
    for copy in over_cols:
        copy.start()
    slots_c[col] = part[...]

    for c in range(chunks):
        arrive(grad_rows(c), down, up)
        for i, out in enumerate((dk_ref, dv_ref)):
            x = centre[c, i, halo : halo + nq, :]
            fill = jnp.zeros((nq - halo, wide), F32)
            x = x + jnp.concatenate([rows_in[c, i, halo : 2 * halo, :].astype(F32), fill], axis=0)
            x = x + jnp.concatenate([fill, rows_in[c, i, 0:halo, :].astype(F32)], axis=0)
            out[:, c * wide : (c + 1) * wide] = x.astype(BF16)
    for copy in over_cols:
        copy.wait()
    total = slots_c[0]
    for k in range(1, n_col):
        total = total + slots_c[k]
    rb_ref[...] = total
    for c in range(chunks):
        sent(key_rows(c), down, up)
        sent(key_cols(c), right, left)
        sent(grad_cols(c), right, left)
        sent(grad_rows(c), down, up)


def shards(n_row, n_col, queries, keys, values, d_out, extents, rel_bias):
    tr, tc, channels = queries.shape
    heads, span = rel_bias.shape[0], rel_bias.shape[1]
    rad = (span - 1) // 2
    nq, nk = tr * tc, tr + 2 * rad
    wide = channels // CHUNKS
    mid, side, halo = nk * tc, nk * (tc // 2), rad * tc
    lanes = -(-((nk + tr - 1) * tc) // 128) * 128
    flat = [x.reshape(nq, channels) for x in (queries, keys, values, d_out)]
    rel = jnp.pad(rel_bias, ((0, 16 - heads), (0, 16 - span), (0, 16 - span))).reshape(16, 256)
    vmem = pl.BlockSpec(memory_space=pltpu.VMEM)
    dma = pltpu.SemaphoreType.DMA
    out = jax.ShapeDtypeStruct((nq, channels), BF16)
    *big, d_rel = pl.pallas_call(
        functools.partial(kernel, n_row, n_col, tr, tc, rad),
        out_shape=[out, out, out, out, jax.ShapeDtypeStruct((16, 256), F32)],
        in_specs=[vmem] * 4 + [pl.BlockSpec(memory_space=pltpu.SMEM), vmem],
        out_specs=[vmem] * 5,
        scratch_shapes=[
            pltpu.VMEM((CHUNKS, 2, mid + 2 * side, wide), BF16),
            pltpu.VMEM((CHUNKS, 2, 2 * side, wide), BF16),
            pltpu.VMEM((channels // 128, mid + 2 * side, 256), F32),
            pltpu.VMEM((nk, 2 * tc, nq), F32),
            pltpu.VMEM((lanes // 128, 16 * 2 * tc, 128), F32),
            pltpu.VMEM((lanes // 128, 16 * 2 * tc, 128), F32),
            pltpu.VMEM((CHUNKS, 2, mid, wide), F32),
            pltpu.VMEM((CHUNKS, 2, 2 * side, wide), BF16),
            pltpu.VMEM((CHUNKS, 2, 2 * side, wide), BF16),
            pltpu.VMEM((CHUNKS, 2, 2 * halo, wide), BF16),
            pltpu.VMEM((CHUNKS, 2, 2 * halo, wide), BF16),
            pltpu.VMEM((16, 256), F32),
            pltpu.VMEM((n_row, 16, 256), F32),
            pltpu.VMEM((n_col, 16, 256), F32),
        ]
        + [dma((CHUNKS, 2))] * 8
        + [dma((n_row,)), dma((n_row,)), dma((n_col,)), dma((n_col,))],
        compiler_params=pltpu.CompilerParams(
            collective_id=0, has_side_effects=True, vmem_limit_bytes=48 * 1024 * 1024
        ),
        cost_estimate=pl.CostEstimate(
            flops=12 * 12 * 128 * 640 * 64, bytes_accessed=8 * 200000, transcendentals=12 * 128 * 640
        ),
    )(*flat, extents, rel)
    big = [x.reshape(tr, tc, channels) for x in big]
    return (*big, d_rel.reshape(16, 16, 16)[:heads, :span, :span])


def solution(mesh):
    tile = P("row", "col", None)
    return jax.shard_map(
        functools.partial(shards, mesh.shape["row"], mesh.shape["col"]),
        mesh=mesh,
        in_specs=(tile, tile, tile, tile, P(), P()),
        out_specs=(tile, tile, tile, tile, P()),
        check_vma=False,
    )
```

profile of v0, /device:TPU:0, one launch (start us, length us, event | category | flops | bytes accessed | tf_op | source)
XLA Modules:
  0.0 52.5 jit_solution(3891864774049520507)
XLA Ops:
  0.6 0.0 copy-start
  0.6 0.9 %pad.4 = f32[16,16,16]{2,1,0:T(8,128)S(1)} pad(f32[12,13,13]{2,1,0:T(8,128)} %param.11, f32[]{:T(128)} %constant.2.clone.1), padding=0_4x0_3x0_3 | pad | bytes 24500 | tf_op jit(solution)/shard_map/jit(_pad)/pad | solution.py:373
  1.6 0.0 copy-start.4
  1.6 0.1 reshape.44.rel_ref
  1.7 0.0 copy-done
  1.7 0.6 %copy-done.4 = s32[2,4,4]{2,1,0:T(4,128)S(1)} copy-done((s32[2,4,4]{2,1,0:T(4,128)S(1)}, s32[2,4,4]{2,1,0:T(4,128)}, u32[]{:S(2)}) %copy-start.4) | copy-done | bytes 152
  2.3 0.0 copy-start.1
  2.3 0.9 %copy-done.1 = bf16[8,16,768]{2,1,0:T(8,128)(2,1)S(1)} copy-done((bf16[8,16,768]{2,1,0:T(8,128)(2,1)S(1)}, bf16[8,16,768]{2,1,0:T(8,128)(2,1)}, u32[]{:S(2)}) %copy-start.1) | copy-done | bytes 196632
  3.2 0.0 copy-start.2
  3.2 0.9 %copy-done.2 = bf16[8,16,768]{2,1,0:T(8,128)(2,1)S(1)} copy-done((bf16[8,16,768]{2,1,0:T(8,128)(2,1)S(1)}, bf16[8,16,768]{2,1,0:T(8,128)(2,1)}, u32[]{:S(2)}) %copy-start.2) | copy-done | bytes 196632
  4.1 0.0 copy-start.3
  4.1 0.9 %copy-done.3 = bf16[8,16,768]{2,1,0:T(8,128)(2,1)S(1)} copy-done((bf16[8,16,768]{2,1,0:T(8,128)(2,1)S(1)}, bf16[8,16,768]{2,1,0:T(8,128)(2,1)}, u32[]{:S(2)}) %copy-start.3) | copy-done | bytes 196632
  5.1 43.9 %shard_map.101 = (bf16[128,768]{1,0:T(8,128)(2,1)S(1)}, bf16[128,768]{1,0:T(8,128)(2,1)S(1)}, bf16[128,768]{1,0:T(8,128)(2,1)S(1)}, bf16[128,768]{1,0:T(8,128)(2,1)S(1)}, f32[16,256]{1,0:T(8,128)S(1)}) custom-call(bf16[128,768]{1,0:T(8,128)(2,1)S(1)} %bitcast.12, bf16[128,768]{1,0:T(8,128)(2,1)S(1)} %bitcast.13, bf16[128,768]{1,0:T(8,128)(2,1)S(1)} %bitcast.14, ...), custom_call_target="tpu_custom_call" | custom-call | flops 754974720 | bytes 1600000 | tf_op jit(solution)/shard_map/pallas_call | solution.py:377
  49.0 0.1 reshape.49
  49.1 0.6 %slice.4 = f32[12,13,13]{2,1,0:T(8,128)} slice(f32[16,16,16]{2,1,0:T(8,128)S(1)} %reshape.49), slice={[0:12], [0:13], [0:13]} | slice | bytes 16224 | tf_op jit(solution)/shard_map/slice | solution.py:408
  49.7 0.7 %copy.15 = bf16[8,16,768]{2,1,0:T(8,128)(2,1)} copy(bf16[8,16,768]{2,1,0:T(8,128)(2,1)S(1)} %bitcast.11) | data formatting | bytes 393216
  50.4 0.7 %copy.16 = bf16[8,16,768]{2,1,0:T(8,128)(2,1)} copy(bf16[8,16,768]{2,1,0:T(8,128)(2,1)S(1)} %bitcast.10) | data formatting | bytes 393216
  51.1 0.7 %copy.17 = bf16[8,16,768]{2,1,0:T(8,128)(2,1)} copy(bf16[8,16,768]{2,1,0:T(8,128)(2,1)S(1)} %bitcast.9) | data formatting | bytes 393216
  51.8 0.7 %copy.18 = bf16[8,16,768]{2,1,0:T(8,128)(2,1)} copy(bf16[8,16,768]{2,1,0:T(8,128)(2,1)S(1)} %bitcast.8) | data formatting | bytes 393216
Async XLA Ops:
  0.6 1.1 %copy-start = (bf16[8,16,768]{2,1,0:T(8,128)(2,1)S(1)}, bf16[8,16,768]{2,1,0:T(8,128)(2,1)}, u32[]{:S(2)}) copy-start(bf16[8,16,768]{2,1,0:T(8,128)(2,1)} %param.6) | copy-start | bytes 589828
  1.6 0.7 %copy-start.4 = (s32[2,4,4]{2,1,0:T(4,128)S(1)}, s32[2,4,4]{2,1,0:T(4,128)}, u32[]{:S(2)}) copy-start(s32[2,4,4]{2,1,0:T(4,128)} %ext_ref.1) | copy-start | bytes 388
  2.3 0.9 %copy-start.1 = (bf16[8,16,768]{2,1,0:T(8,128)(2,1)S(1)}, bf16[8,16,768]{2,1,0:T(8,128)(2,1)}, u32[]{:S(2)}) copy-start(bf16[8,16,768]{2,1,0:T(8,128)(2,1)} %param.7) | copy-start | bytes 589828
  3.2 0.9 %copy-start.2 = (bf16[8,16,768]{2,1,0:T(8,128)(2,1)S(1)}, bf16[8,16,768]{2,1,0:T(8,128)(2,1)}, u32[]{:S(2)}) copy-start(bf16[8,16,768]{2,1,0:T(8,128)(2,1)} %param.8) | copy-start | bytes 589828
  4.1 0.9 %copy-start.3 = (bf16[8,16,768]{2,1,0:T(8,128)(2,1)S(1)}, bf16[8,16,768]{2,1,0:T(8,128)(2,1)}, u32[]{:S(2)}) copy-start(bf16[8,16,768]{2,1,0:T(8,128)(2,1)} %param.9) | copy-start | bytes 589828
where the time goes:
time: 52.7 us; the launch traced here: 52.5 us
  Pallas kernels  43.9 us (83%)
  local copies, waits for them, and re-layouts  7.85 us (15%)
  between operations  0.68 us (1%)
    pallas_call x1, Pallas kernels, shards(): pl.pallas_call(functools.partial(kernel, n_row, n_col, tr, tc, rad), out_...  43.9 us
    unnamed x14, local copies, waits for them, and re-layouts  6.05 us

commit v1 on v0

--- a/solution.py
+++ b/solution.py
@@ -10,7 +10,7 @@
 MESH = pl.DeviceIdType.MESH
 F32 = jnp.float32
 BF16 = jnp.bfloat16
-CHUNKS = 3
+CHUNKS = 6
 NEG = -1e30
 
 
@@ -30,11 +30,11 @@
 
 def kernel(
     n_row, n_col, tr, tc, rad,
-    q_ref, k_ref, v_ref, g_ref, ext_ref, rel_ref,
+    q_hbm, k_hbm, v_hbm, g_hbm, ext_ref, rel_ref,
     o_ref, dq_ref, dk_ref, dv_ref, rb_ref,
-    kv, pack, bias, mask, table, dtable, centre, strip_out, strip_in, rows_out, rows_in,
+    q_ref, g_ref, kv, pack, bias, mask, rel_pad, turned, table, dtable, centre, strip_out, strip_in, rows_out, rows_in,
     part, slots_r, slots_c,
-    kr_s, kr_r, kc_s, kc_r, gc_s, gc_r, gr_s, gr_r, br_s, br_r, bc_s, bc_r,
+    in_sem, kr_s, kr_r, kc_s, kc_r, gc_s, gc_r, gr_s, gr_r, br_s, br_r, bc_s, bc_r,
 ):
     row, col = lax.axis_index("row"), lax.axis_index("col")
     nk = tr + 2 * rad
@@ -45,7 +45,7 @@
     chunks, _, keys, wide = kv.shape
     per = wide // 128
     pairs = chunks * per
-    panels_r, panels_c = ext_ref.shape[1], ext_ref.shape[2]
+    panels_c = ext_ref.shape[2]
     panel = 2 * tr
 
     up, down = row > 0, row < n_row - 1
@@ -53,6 +53,21 @@
     row_down, row_up = lax.rem(row + 1, n_row), lax.rem(row + n_row - 1, n_row)
     col_right, col_left = lax.rem(col + 1, n_col), lax.rem(col + n_col - 1, n_col)
 
+    loads = [
+        pltpu.make_async_copy(
+            source.at[:, c * wide : (c + 1) * wide],
+            kv.at[c, i, halo : halo + nq],
+            in_sem.at[2 * c + i],
+        )
+        for c in range(chunks)
+        for i, source in enumerate((k_hbm, v_hbm))
+    ]
+    late = [
+        pltpu.make_async_copy(q_hbm, q_ref, in_sem.at[2 * chunks]),
+        pltpu.make_async_copy(g_hbm, g_ref, in_sem.at[2 * chunks + 1]),
+    ]
+    for copy in loads + late:
+        copy.start()
     barrier = pltpu.get_barrier_semaphore()
     for step in range(1, n_row):
         pl.semaphore_signal(
@@ -63,9 +78,8 @@
             barrier, inc=1, device_id=(row, lax.rem(col + step, n_col)), device_id_type=MESH
         )
 
-    for c in range(chunks):
-        kv[c, 0, halo : halo + nq, :] = k_ref[:, c * wide : (c + 1) * wide]
-        kv[c, 1, halo : halo + nq, :] = v_ref[:, c * wide : (c + 1) * wide]
+    for copy in loads:
+        copy.wait()
     pl.semaphore_wait(barrier, n_row - 1 + n_col - 1)
 
     def remote(src, dst, send, recv, to):
@@ -141,28 +155,27 @@
         strip_in[:, :, 0:side, :] = jnp.zeros((chunks, 2, side, wide), BF16)
 
     tiles_n = table.shape[0]
-    span_lanes = tiles_n * 128
-    heads_pad = rel_ref.shape[0]
     cols2 = 2 * tc
-
-    def one_hot(kc):
-        lane = lax.broadcasted_iota(jnp.int32, (1, span_lanes), 1)
-        a = nk - 1 - lane // tc
-        b = kc - (half - rad) - lane % tc
-        target = jnp.where((a >= 0) & (a < 16) & (b >= 0) & (b < 16), a * 16 + b, -1)
-        place = lax.broadcasted_iota(jnp.int32, (256, span_lanes), 0)
-        return jnp.where(place == target, 1.0, 0.0).astype(BF16)
-
-    rel2 = halves(rel_ref[...])
-
-    def fill_table(kc, carry):
-        both = nn(rel2, one_hot(kc))
-        both = both[:heads_pad] + both[heads_pad:]
+    fit = 128 // cols2
+    groups = pairs * 2 // fit
+    span = 2 * rad + 1
+    edge = half - rad
+    rel_pad[...] = jnp.zeros_like(rel_pad)
+
+    def fill_rel(a, carry):
+        for h in range(pairs * 2):
+            at = (h % fit) * cols2
+            rel_pad[h // fit, pl.ds(nk - 1 - a, 1), at : at + span] = rel_ref[h, pl.ds(a, 1), :]
+        return carry
+
+    lax.fori_loop(0, span, fill_rel, 0)
+    steps = tiles_n * 128 // tc
+    for g in range(groups):
+        x = rel_pad[g]
+        for qc in range(tc):
+            turned[g, pl.ds(qc, steps, stride=tc), :] = pltpu.roll(x, qc + edge, 1)
         for t in range(tiles_n):
-            table[t, pl.ds(kc, heads_pad, stride=cols2), :] = both[:, t * 128 : (t + 1) * 128]
-        return carry
-
-    lax.fori_loop(0, cols2, fill_table, 0)
+            table[t, g * 128 : (g + 1) * 128, :] = turned[g, t * 128 : (t + 1) * 128, :].T
 
     sub = lax.broadcasted_iota(jnp.int32, (cols2, nq), 0)
     lane = lax.broadcasted_iota(jnp.int32, (cols2, nq), 1)
@@ -232,8 +245,8 @@
 
     def compute(c, pp):
         p = c * per + pp
-        at = pl.multiple_of(pp * 128, 128)
-        full = pl.multiple_of(p * 128, 128)
+        at = pp * 128
+        full = p * 128
         k2 = kv[c, 0, :, pl.ds(at, 128)]
         v2 = kv[c, 1, :, pl.ds(at, 128)]
         qb = block(q_ref[:, pl.ds(full, 128)].astype(F32) * 0.125)
@@ -291,31 +304,27 @@
             centre[c, i, halo : halo + nq, :] = total[halo : halo + nq]
         start(grad_rows(c), down, up)
 
+    for copy in late:
+        copy.wait()
     send_cols(0)
     for c in range(chunks):
         if c + 1 < chunks:
             send_cols(c + 1)
         arrive(key_cols(c), right, left)
 
-        def one(pp, carry, c=c):
+        for pp in range(per):
             compute(c, pp)
-            return carry
-
-        lax.fori_loop(0, per, one, 0)
         start(grad_cols(c), right, left)
         if c:
             send_rows(c - 1)
-    unused = heads_pad - pairs * 2
-    dtable[:, pairs * 2 * cols2 :, :] = jnp.zeros((tiles_n, unused * cols2, 128), F32)
-
-    def gather_bias(kc, total):
-        x = jnp.concatenate(
-            [dtable[t, pl.ds(kc, heads_pad, stride=cols2), :] for t in range(tiles_n)], axis=1
-        )
-        both = nt(halves(x), one_hot(kc))
-        return total + both[:heads_pad] + both[heads_pad:]
-
-    part[...] = lax.fori_loop(0, cols2, gather_bias, jnp.zeros((heads_pad, 256), F32))
+    for g in range(groups):
+        for t in range(tiles_n):
+            turned[g, t * 128 : (t + 1) * 128, :] = dtable[t, g * 128 : (g + 1) * 128, :].T
+        total = jnp.zeros((16, 128), F32)
+        for qc in range(tc):
+            x = turned[g, pl.ds((tr - 1) * tc + qc, 16, stride=tc), :]
+            total = total + pltpu.roll(x, 128 - qc - edge, 1)
+        part[g * 16 : (g + 1) * 16, :] = total
 
     def spread(slots, me, count, send, recv, to):
         copies = [
@@ -353,12 +362,32 @@
     total = slots_c[0]
     for k in range(1, n_col):
         total = total + slots_c[k]
-    rb_ref[...] = total
+    part[...] = total
+
+    def give_rel(a, carry):
+        for h in range(pairs * 2):
+            at = (h % fit) * cols2
+            row_at = h // fit * 16 + 2 * rad - a
+            rb_ref[h, pl.ds(a, 1), :] = part[pl.ds(row_at, 1), at : at + span]
+        return carry
+
+    lax.fori_loop(0, span, give_rel, 0)
     for c in range(chunks):
         sent(key_rows(c), down, up)
         sent(key_cols(c), right, left)
         sent(grad_cols(c), right, left)
         sent(grad_rows(c), down, up)
+
+
+def hand_over(*refs):
+    sems = refs[-1]
+    copies = [
+        pltpu.make_async_copy(refs[i], refs[4 + i], sems.at[i]) for i in range(4)
+    ]
+    for copy in copies:
+        copy.start()
+    for copy in copies:
+        copy.wait()
 
 
 def shards(n_row, n_col, queries, keys, values, d_out, extents, rel_bias):
@@ -368,44 +397,57 @@
     nq, nk = tr * tc, tr + 2 * rad
     wide = channels // CHUNKS
     mid, side, halo = nk * tc, nk * (tc // 2), rad * tc
+    groups = heads * 2 * tc // 128
     lanes = -(-((nk + tr - 1) * tc) // 128) * 128
     flat = [x.reshape(nq, channels) for x in (queries, keys, values, d_out)]
-    rel = jnp.pad(rel_bias, ((0, 16 - heads), (0, 16 - span), (0, 16 - span))).reshape(16, 256)
     vmem = pl.BlockSpec(memory_space=pltpu.VMEM)
+    hbm = pl.BlockSpec(memory_space=pltpu.HBM)
     dma = pltpu.SemaphoreType.DMA
     out = jax.ShapeDtypeStruct((nq, channels), BF16)
     *big, d_rel = pl.pallas_call(
         functools.partial(kernel, n_row, n_col, tr, tc, rad),
-        out_shape=[out, out, out, out, jax.ShapeDtypeStruct((16, 256), F32)],
-        in_specs=[vmem] * 4 + [pl.BlockSpec(memory_space=pltpu.SMEM), vmem],
+        out_shape=[out, out, out, out, jax.ShapeDtypeStruct(rel_bias.shape, F32)],
+        in_specs=[hbm] * 4 + [pl.BlockSpec(memory_space=pltpu.SMEM), vmem],
         out_specs=[vmem] * 5,
         scratch_shapes=[
+            pltpu.VMEM((nq, channels), BF16),
+            pltpu.VMEM((nq, channels), BF16),
             pltpu.VMEM((CHUNKS, 2, mid + 2 * side, wide), BF16),
             pltpu.VMEM((CHUNKS, 2, 2 * side, wide), BF16),
             pltpu.VMEM((channels // 128, mid + 2 * side, 256), F32),
             pltpu.VMEM((nk, 2 * tc, nq), F32),
-            pltpu.VMEM((lanes // 128, 16 * 2 * tc, 128), F32),
-            pltpu.VMEM((lanes // 128, 16 * 2 * tc, 128), F32),
+            pltpu.VMEM((groups, lanes // tc, 128), F32),
+            pltpu.VMEM((groups, lanes, 128), F32),
+            pltpu.VMEM((lanes // 128, heads * 2 * tc, 128), F32),
+            pltpu.VMEM((lanes // 128, heads * 2 * tc, 128), F32),
             pltpu.VMEM((CHUNKS, 2, mid, wide), F32),
             pltpu.VMEM((CHUNKS, 2, 2 * side, wide), BF16),
             pltpu.VMEM((CHUNKS, 2, 2 * side, wide), BF16),
             pltpu.VMEM((CHUNKS, 2, 2 * halo, wide), BF16),
             pltpu.VMEM((CHUNKS, 2, 2 * halo, wide), BF16),
-            pltpu.VMEM((16, 256), F32),
-            pltpu.VMEM((n_row, 16, 256), F32),
-            pltpu.VMEM((n_col, 16, 256), F32),
+            pltpu.VMEM((groups * 16, 128), F32),
+            pltpu.VMEM((n_row, groups * 16, 128), F32),
+            pltpu.VMEM((n_col, groups * 16, 128), F32),
         ]
+        + [dma((2 * CHUNKS + 2,))]
         + [dma((CHUNKS, 2))] * 8
         + [dma((n_row,)), dma((n_row,)), dma((n_col,)), dma((n_col,))],
         compiler_params=pltpu.CompilerParams(
-            collective_id=0, has_side_effects=True, vmem_limit_bytes=48 * 1024 * 1024
+            collective_id=0, has_side_effects=True, vmem_limit_bytes=63 * 1024 * 1024
         ),
         cost_estimate=pl.CostEstimate(
             flops=12 * 12 * 128 * 640 * 64, bytes_accessed=8 * 200000, transcendentals=12 * 128 * 640
         ),
-    )(*flat, extents, rel)
-    big = [x.reshape(tr, tc, channels) for x in big]
-    return (*big, d_rel.reshape(16, 16, 16)[:heads, :span, :span])
+    )(*flat, extents, rel_bias)
+    anywhere = pl.BlockSpec(memory_space=pl.ANY)
+    big = pl.pallas_call(
+        hand_over,
+        out_shape=[out] * 4,
+        in_specs=[anywhere] * 4,
+        out_specs=[hbm] * 4,
+        scratch_shapes=[dma((4,))],
+    )(*big)
+    return (*(x.reshape(tr, tc, channels) for x in big), d_rel)
 
 
 def solution(mesh):

time: 52.7 us -> 71.2 us (1.35)
  Pallas kernels: 43.9 us -> 69.7 us
  local copies, waits for them, and re-layouts: 7.85 us -> 0.65 us
    pallas_call x0 -> x1, Pallas kernels: none -> 25 us  [shards(): pl.pallas_call(hand_over, out_shape=[out] * 4, in_specs=[anywhere] * 4, o...]
    unnamed x14 -> x3, local copies, waits for them, and re-layouts: 6.05 us -> 0.65 us
    pad x1 -> x0, local copies, waits for them, and re-layouts: 0.95 us -> none  [shards(): jnp.pad(rel_bias, ((0, 16 - heads), (0, 16 - span), (0, 16 - span)))]
    pallas_call x1, Pallas kernels: 43.9 us -> 44.7 us  [shards(): pl.pallas_call(functools.partial(kernel, n_row, n_col, tr, tc, rad), out_...]
where the time goes in v1:
time: 71.2 us; the launch traced here: 71 us
  Pallas kernels  69.7 us (98%)
    pallas_call x1, Pallas kernels, shards(): pl.pallas_call(functools.partial(kernel, n_row, n_col, tr, tc, rad), out_...  44.7 us
    pallas_call x1, Pallas kernels, shards(): pl.pallas_call(hand_over, out_shape=[out] * 4, in_specs=[anywhere] * 4, o...  25 us

profile of v1, /device:TPU:0, one launch (start us, length us, event | category | flops | bytes accessed | tf_op | source)
XLA Modules:
  0.0 71.0 jit_solution(1714806438159339378)
XLA Ops:
  0.6 44.7 %shard_map.101 = (bf16[128,768]{1,0:T(8,128)(2,1)}, bf16[128,768]{1,0:T(8,128)(2,1)}, bf16[128,768]{1,0:T(8,128)(2,1)}, bf16[128,768]{1,0:T(8,128)(2,1)}, f32[12,13,13]{2,1,0:T(8,128)}) custom-call(bf16[128,768]{1,0:T(8,128)(2,1)} %bitcast.8, bf16[128,768]{1,0:T(8,128)(2,1)} %bitcast.9, bf16[128,768]{1,0:T(8,128)(2,1)} %bitcast.10, ...), custom_call_target="tpu_custom_call" | custom-call | flops 754974720 | bytes 1600000 | tf_op jit(solution)/shard_map/pallas_call | solution.py:407
  45.4 0.0 copy-start
  45.4 25.0 %shard_map.102 = (bf16[128,768]{1,0:T(8,128)(2,1)}, bf16[128,768]{1,0:T(8,128)(2,1)}, bf16[128,768]{1,0:T(8,128)(2,1)}, bf16[128,768]{1,0:T(8,128)(2,1)}) custom-call(bf16[128,768]{1,0:T(8,128)(2,1)} %get-tuple-element.14.refs_0_, bf16[128,768]{1,0:T(8,128)(2,1)} %get-tuple-element.15.refs_1_, bf16[128,768]{1,0:T(8,128)(2,1)} %get-tuple-element.16.refs_2_, ...), custom_call_target="tpu_custom_call" | custom-call | tf_op jit(solution)/shard_map/pallas_call | solution.py:443
  70.4 0.0 copy-done
  70.4 0.6 copy.12
Async XLA Ops:
  45.4 25.0 %copy-start = (f32[12,13,13]{2,1,0:T(8,128)S(1)}, f32[12,13,13]{2,1,0:T(8,128)}, u32[]{:S(2)}) copy-start(f32[12,13,13]{2,1,0:T(8,128)} %get-tuple-element.32) | copy-start | bytes 24340

commit v2 on v1

--- a/solution.py
+++ b/solution.py
@@ -78,8 +78,6 @@
             barrier, inc=1, device_id=(row, lax.rem(col + step, n_col)), device_id_type=MESH
         )
 
-    for copy in loads:
-        copy.wait()
     pl.semaphore_wait(barrier, n_row - 1 + n_col - 1)
 
     def remote(src, dst, send, recv, to):
@@ -131,8 +129,13 @@
         pl.when(after)(lambda: copies[0].wait_send())
         pl.when(before)(lambda: copies[1].wait_send())
 
-    for c in range(chunks):
+    def send_keys(c):
+        loads[2 * c].wait()
+        loads[2 * c + 1].wait()
         start(key_rows(c), down, up)
+
+    for c in range(min(2, chunks)):
+        send_keys(c)
 
     @pl.when(jnp.logical_not(up))
     def _():
@@ -231,6 +234,8 @@
 
     def send_cols(c):
         arrive(key_rows(c), down, up)
+        if c + 2 < chunks:
+            send_keys(c + 2)
         for i in range(2):
             x = kv[c, i, 0:mid, :].astype(F32).reshape(nk, tc, wide)
             pack[c, i, 0:side, :] = x[:, half:].reshape(side, wide).astype(BF16)
@@ -271,24 +276,30 @@
             strip_out[c, i, :, pl.ds(at, 128)] = grad[mid:].astype(BF16)
         for hh in range(2):
             d = ds[:, hh * 128 : (hh + 1) * 128]
-            sums = [jnp.zeros((cols2, nq), F32) for _ in range(tiles_n)]
-            for kr in range(nk):
-                off = (nk - 1 - kr) * tc
-                t, s = off // 128, off % 128
-                at2 = mid + kr * half
-                x = jnp.concatenate(
-                    [d[at2 : at2 + half], d[kr * tc : (kr + 1) * tc],
-                     d[side + at2 : side + at2 + half]], axis=0,
-                )
-                if s:
-                    x = pltpu.roll(x, s, 1)
-                    sums[t] = sums[t] + jnp.where(lane >= s, x, 0.0)
-                    sums[t + 1] = sums[t + 1] + jnp.where(lane >= s, 0.0, x)
+            even, odd = jnp.zeros((cols2, nq), F32), jnp.zeros((cols2, nq), F32)
+            for turn in range(128 // tc):
+                both = [None, None]
+                for kr in range(nk):
+                    place = nk - 1 - kr
+                    if place % (128 // tc) != turn:
+                        continue
+                    at2 = mid + kr * half
+                    x = jnp.concatenate(
+                        [d[at2 : at2 + half], d[kr * tc : (kr + 1) * tc],
+                         d[side + at2 : side + at2 + half]], axis=0,
+                    )
+                    i = place // (128 // tc) % 2
+                    both[i] = x if both[i] is None else both[i] + x
+                shift = turn * tc
+                if shift:
+                    one, two = (pltpu.roll(x, shift, 1) for x in both)
+                    even = even + jnp.where(lane >= shift, one, two)
+                    odd = odd + jnp.where(lane >= shift, two, one)
                 else:
-                    sums[t] = sums[t] + x
-            base = pl.multiple_of((p * 2 + hh) * cols2, cols2)
-            for t, total in enumerate(sums):
-                dtable[t, pl.ds(base, cols2), :] = total
+                    even, odd = even + both[0], odd + both[1]
+            base = (p * 2 + hh) * cols2
+            dtable[0, base : base + cols2, :] = even
+            dtable[1, base : base + cols2, :] = odd
 
     def send_rows(c):
         arrive(grad_cols(c), right, left)
@@ -306,48 +317,60 @@
 
     for copy in late:
         copy.wait()
+    def spread(g, slots, me, count, send, recv, to):
+        return [
+            remote(part.at[g], slots.at[g, me], send.at[g, k], recv.at[g, k],
+                   to(lax.rem(me + k, count)))
+            for k in range(1, count)
+        ]
+
+    def over_rows(g):
+        return spread(g, slots_r, row, n_row, br_s, br_r, lambda k: (k, col))
+
+    def over_cols(g):
+        return spread(g, slots_c, col, n_col, bc_s, bc_r, lambda k: (row, k))
+
+    def gather_bias(g):
+        for t in range(2):
+            turned[g, t * 128 : (t + 1) * 128, :] = dtable[t, g * 128 : (g + 1) * 128, :].T
+        total = jnp.zeros((16, 128), F32)
+        for qc in range(tc):
+            x = turned[g, pl.ds(qc, 16, stride=tc), :]
+            total = total + pltpu.roll(x, 128 - qc - edge, 1)
+        part[g] = total
+        for copy in over_rows(g):
+            copy.start()
+        slots_r[g, row] = total
+
+    def turn_bias(g):
+        for copy in over_rows(g):
+            copy.wait()
+        total = slots_r[g, 0]
+        for k in range(1, n_row):
+            total = total + slots_r[g, k]
+        part[g] = total
+        for copy in over_cols(g):
+            copy.start()
+        slots_c[g, col] = total
+
+    group_pairs = fit // 2
     send_cols(0)
     for c in range(chunks):
         if c + 1 < chunks:
             send_cols(c + 1)
         arrive(key_cols(c), right, left)
-
         for pp in range(per):
             compute(c, pp)
         start(grad_cols(c), right, left)
         if c:
             send_rows(c - 1)
-    for g in range(groups):
-        for t in range(tiles_n):
-            turned[g, t * 128 : (t + 1) * 128, :] = dtable[t, g * 128 : (g + 1) * 128, :].T
-        total = jnp.zeros((16, 128), F32)
-        for qc in range(tc):
-            x = turned[g, pl.ds((tr - 1) * tc + qc, 16, stride=tc), :]
-            total = total + pltpu.roll(x, 128 - qc - edge, 1)
-        part[g * 16 : (g + 1) * 16, :] = total
-
-    def spread(slots, me, count, send, recv, to):
-        copies = [
-            remote(part, slots.at[me], send.at[k], recv.at[k], to(lax.rem(me + k, count)))
-            for k in range(1, count)
-        ]
-        return copies
-
-    over_rows = spread(slots_r, row, n_row, br_s, br_r, lambda r: (r, col))
-    for copy in over_rows:
-        copy.start()
-    slots_r[row] = part[...]
+        done = (c + 1) * per
+        if done % group_pairs == 0:
+            gather_bias(done // group_pairs - 1)
+        elif done // group_pairs:
+            turn_bias(done // group_pairs - 1)
     send_rows(chunks - 1)
-    for copy in over_rows:
-        copy.wait()
-    total = slots_r[0]
-    for k in range(1, n_row):
-        total = total + slots_r[k]
-    part[...] = total
-    over_cols = spread(slots_c, col, n_col, bc_s, bc_r, lambda k: (row, k))
-    for copy in over_cols:
-        copy.start()
-    slots_c[col] = part[...]
+    turn_bias(groups - 1)
 
     for c in range(chunks):
         arrive(grad_rows(c), down, up)
@@ -357,18 +380,19 @@
             x = x + jnp.concatenate([rows_in[c, i, halo : 2 * halo, :].astype(F32), fill], axis=0)
             x = x + jnp.concatenate([fill, rows_in[c, i, 0:halo, :].astype(F32)], axis=0)
             out[:, c * wide : (c + 1) * wide] = x.astype(BF16)
-    for copy in over_cols:
-        copy.wait()
-    total = slots_c[0]
-    for k in range(1, n_col):
-        total = total + slots_c[k]
-    part[...] = total
+    for g in range(groups):
+        for copy in over_cols(g):
+            copy.wait()
+        total = slots_c[g, 0]
+        for k in range(1, n_col):
+            total = total + slots_c[g, k]
+        part[g] = total
 
     def give_rel(a, carry):
         for h in range(pairs * 2):
             at = (h % fit) * cols2
-            row_at = h // fit * 16 + 2 * rad - a
-            rb_ref[h, pl.ds(a, 1), :] = part[pl.ds(row_at, 1), at : at + span]
+            row_at = lax.rem(nk - 1 - a, 16)
+            rb_ref[h, pl.ds(a, 1), :] = part[h // fit, pl.ds(row_at, 1), at : at + span]
         return carry
 
     lax.fori_loop(0, span, give_rel, 0)
@@ -380,13 +404,15 @@
 
 
 def hand_over(*refs):
-    sems = refs[-1]
-    copies = [
-        pltpu.make_async_copy(refs[i], refs[4 + i], sems.at[i]) for i in range(4)
-    ]
-    for copy in copies:
+    sources, targets, (held, sems) = refs[:4], refs[4:8], refs[8:]
+    first = [pltpu.make_async_copy(sources[i], held.at[i], sems.at[0, i]) for i in range(4)]
+    second = [pltpu.make_async_copy(held.at[i], targets[i], sems.at[1, i]) for i in range(4)]
+    for copy in first:
         copy.start()
-    for copy in copies:
+    for before, after in zip(first, second):
+        before.wait()
+        after.start()
+    for copy in second:
         copy.wait()
 
 
@@ -419,19 +445,20 @@
             pltpu.VMEM((groups, lanes // tc, 128), F32),
             pltpu.VMEM((groups, lanes, 128), F32),
             pltpu.VMEM((lanes // 128, heads * 2 * tc, 128), F32),
-            pltpu.VMEM((lanes // 128, heads * 2 * tc, 128), F32),
+            pltpu.VMEM((2, heads * 2 * tc, 128), F32),
             pltpu.VMEM((CHUNKS, 2, mid, wide), F32),
             pltpu.VMEM((CHUNKS, 2, 2 * side, wide), BF16),
             pltpu.VMEM((CHUNKS, 2, 2 * side, wide), BF16),
             pltpu.VMEM((CHUNKS, 2, 2 * halo, wide), BF16),
             pltpu.VMEM((CHUNKS, 2, 2 * halo, wide), BF16),
-            pltpu.VMEM((groups * 16, 128), F32),
-            pltpu.VMEM((n_row, groups * 16, 128), F32),
-            pltpu.VMEM((n_col, groups * 16, 128), F32),
+            pltpu.VMEM((groups, 16, 128), F32),
+            pltpu.VMEM((groups, n_row, 16, 128), F32),
+            pltpu.VMEM((groups, n_col, 16, 128), F32),
         ]
         + [dma((2 * CHUNKS + 2,))]
         + [dma((CHUNKS, 2))] * 8
-        + [dma((n_row,)), dma((n_row,)), dma((n_col,)), dma((n_col,))],
+        + [dma((groups, n_row))] * 2
+        + [dma((groups, n_col))] * 2,
         compiler_params=pltpu.CompilerParams(
             collective_id=0, has_side_effects=True, vmem_limit_bytes=63 * 1024 * 1024
         ),
@@ -439,13 +466,13 @@
             flops=12 * 12 * 128 * 640 * 64, bytes_accessed=8 * 200000, transcendentals=12 * 128 * 640
         ),
     )(*flat, extents, rel_bias)
-    anywhere = pl.BlockSpec(memory_space=pl.ANY)
     big = pl.pallas_call(
         hand_over,
         out_shape=[out] * 4,
-        in_specs=[anywhere] * 4,
+        in_specs=[hbm] * 4,
         out_specs=[hbm] * 4,
-        scratch_shapes=[dma((4,))],
+        scratch_shapes=[pltpu.VMEM((4, nq, channels), BF16), dma((2, 4))],
+        compiler_params=pltpu.CompilerParams(vmem_limit_bytes=63 * 1024 * 1024),
     )(*big)
     return (*(x.reshape(tr, tc, channels) for x in big), d_rel)
 

time: 71.2 us -> 47.1 us (0.66)
  Pallas kernels: 69.7 us -> 45.6 us
    pallas_call x1, Pallas kernels: 25 us -> 1.99 us  [shards(): pl.pallas_call(hand_over, out_shape=[out] * 4, in_specs=[hbm] * 4, out_sp...]
    pallas_call x1, Pallas kernels: 44.7 us -> 43.6 us  [shards(): pl.pallas_call(functools.partial(kernel, n_row, n_col, tr, tc, rad), out_...]
where the time goes in v2:
time: 47.1 us; the launch traced here: 46.9 us
  Pallas kernels  45.6 us (97%)
  between operations  0.66 us (1%)
  local copies, waits for them, and re-layouts  0.65 us (1%)
    pallas_call x1, Pallas kernels, shards(): pl.pallas_call(functools.partial(kernel, n_row, n_col, tr, tc, rad), out_...  43.6 us
    pallas_call x1, Pallas kernels, shards(): pl.pallas_call(hand_over, out_shape=[out] * 4, in_specs=[hbm] * 4, out_sp...  1.99 us

profile of v2, /device:TPU:0, one launch (start us, length us, event | category | flops | bytes accessed | tf_op | source)
XLA Modules:
  0.0 46.9 jit_solution(6786306777998839282)
XLA Ops:
  0.6 43.6 %shard_map.101 = (bf16[128,768]{1,0:T(8,128)(2,1)}, bf16[128,768]{1,0:T(8,128)(2,1)}, bf16[128,768]{1,0:T(8,128)(2,1)}, bf16[128,768]{1,0:T(8,128)(2,1)}, f32[12,13,13]{2,1,0:T(8,128)}) custom-call(bf16[128,768]{1,0:T(8,128)(2,1)} %bitcast.8, bf16[128,768]{1,0:T(8,128)(2,1)} %bitcast.9, bf16[128,768]{1,0:T(8,128)(2,1)} %bitcast.10, ...), custom_call_target="tpu_custom_call" | custom-call | flops 754974720 | bytes 1600000 | tf_op jit(solution)/shard_map/pallas_call | solution.py:433
  44.2 0.0 copy-start
  44.2 2.0 %shard_map.102 = (bf16[128,768]{1,0:T(8,128)(2,1)}, bf16[128,768]{1,0:T(8,128)(2,1)}, bf16[128,768]{1,0:T(8,128)(2,1)}, bf16[128,768]{1,0:T(8,128)(2,1)}) custom-call(bf16[128,768]{1,0:T(8,128)(2,1)} %get-tuple-element.14.refs_0_, bf16[128,768]{1,0:T(8,128)(2,1)} %get-tuple-element.15.refs_1_, bf16[128,768]{1,0:T(8,128)(2,1)} %get-tuple-element.16.refs_2_, ...), custom_call_target="tpu_custom_call" | custom-call | tf_op jit(solution)/shard_map/pallas_call | solution.py:469
  46.2 0.0 copy-done
  46.3 0.6 %copy.12 = f32[12,13,13]{2,1,0:T(8,128)} copy(f32[12,13,13]{2,1,0:T(8,128)S(1)} %copy-done) | data formatting | bytes 16224
Async XLA Ops:
  44.2 2.0 %copy-start = (f32[12,13,13]{2,1,0:T(8,128)S(1)}, f32[12,13,13]{2,1,0:T(8,128)}, u32[]{:S(2)}) copy-start(f32[12,13,13]{2,1,0:T(8,128)} %get-tuple-element.32) | copy-start | bytes 24340
